TPU v7x, 256 devices: a whole 4x4x8 slice. The times are simulated.
256 devices in a mesh: segment: 8 (over x, z_lo), expert: 32 (over y, z_hi, core).
Axes of the slice: x: 4, y: 4, z: 8 (z_hi: 4, z_lo: 2; z = z_hi * 2 + z_lo), core: 2. Of those that a mesh axis runs over, the one named last changes fastest.
Arguments:
- fwd_prev: bfloat16 [8, 2048, 1536], P('segment', 'expert'), may hold values from -6 to 6
- bwd_prev: bfloat16 [8, 2048, 1536], P('segment', 'expert'), may hold values from -6 to 6
- stored_in: bfloat16 [8, 2048, 1536], P('segment', 'expert'), may hold values from -6 to 6
- fwd_routes: int32 [8, 2048, 4], P('segment', 'expert'), may hold values from 0 to 31, all different within a row; in each aligned block of 64 rows (0 to 63, 64 to 127, ..., all dimensions but the last counted through in order) at most 16 rows name the same one
- fwd_gates: float32 [8, 2048, 4], P('segment', 'expert'), may hold values from 0.05 to 1
- bwd_routes: int32 [8, 2048, 4], P('segment', 'expert'), may hold values from 0 to 31, all different within a row; in each aligned block of 64 rows (0 to 63, 64 to 127, ..., all dimensions but the last counted through in order) at most 16 rows name the same one
- bwd_gates: float32 [8, 2048, 4], P('segment', 'expert'), may hold values from 0.05 to 1
- norm_gain: float32 [8, 1536], P('segment'), may hold values from 0.1 to 1.9
- w_up: bfloat16 [8, 32, 1536, 1536], P('segment', 'expert'), may hold values from -0.15625 to 0.15625
- w_down: bfloat16 [8, 32, 1536, 1536], P('segment', 'expert'), may hold values from -0.15625 to 0.15625
Outputs:
- fwd_out: bfloat16 [8, 2048, 1536], P('segment', 'expert')
- bwd_out: bfloat16 [8, 2048, 1536], P('segment', 'expert')
Inputs may be any that keep to these rules, and one draw needn't show every extreme that they name: `fwd_routes`: the 4 ids of a token differ. In each aligned block of 64 tokens of a segment (the tokens of one device), no expert is named by more than 16 tokens, a bound that some block reaches. `bwd_routes`: the 4 ids of a token differ. In each aligned block of 64 tokens of a segment (the tokens of one device), no expert is named by more than 16 tokens, a bound that some block reaches.
All inputs are finite; a program needn't handle non-finite values.
Results may differ from a plain program's by a relative error of at most 0.0048.
Values may be sent and summed in bfloat16 or wider, within the bound.
A program may use at most 64 MiB of HBM per device.

v0:
```python
import jax
import jax.numpy as jnp
from jax import lax
from jax.sharding import PartitionSpec as P

TOP = 4
MOST = 16


norm_eps = 1e-05


def passed_along(value, axis, steps):
    count = lax.axis_size(axis)
    pairs = [(source, (source + steps) % count) for source in range(count)]
    return lax.ppermute(value, axis, pairs)


def normalize(rows, gain):
    values = rows.astype(jnp.float32)
    scale = lax.rsqrt(jnp.mean(values * values, axis=-1, keepdims=True) + norm_eps)
    return (values, scale, (values * scale * gain).astype(jnp.bfloat16))


def expert_forward(rows, up_weight, down_weight):
    pre = jnp.dot(rows, up_weight, preferred_element_type=jnp.float32)
    act = jax.nn.silu(pre).astype(jnp.bfloat16)
    return jnp.dot(act, down_weight, preferred_element_type=jnp.float32).astype(jnp.bfloat16)


def expert_backward(rows, cotan, up_weight, down_weight):
    pre = jnp.dot(rows, up_weight, preferred_element_type=jnp.float32)
    sigma = jax.nn.sigmoid(pre)
    deriv = sigma * (1.0 + pre * (1.0 - sigma))
    back = lax.dot_general(
        cotan, down_weight, (((1,), (1,)), ((), ())), preferred_element_type=jnp.float32
    )
    inner = (back * deriv).astype(jnp.bfloat16)
    return lax.dot_general(
        inner, up_weight, (((1,), (1,)), ((), ())), preferred_element_type=jnp.float32
    ).astype(jnp.bfloat16)


def slot_index(routes, experts):
    flat = routes.reshape(-1)
    onehot = (flat[:, None] == jnp.arange(experts, dtype=jnp.int32)[None, :]).astype(jnp.int32)
    rank = jnp.sum((jnp.cumsum(onehot, axis=0) - onehot) * onehot, axis=1)
    return flat * MOST + rank


def pack_rows(rows, dest, experts):
    buffer = jnp.zeros((experts * MOST, rows.shape[1]), rows.dtype)
    buffer = buffer.at[dest].set(jnp.repeat(rows, TOP, axis=0))
    return buffer.reshape(experts, MOST, rows.shape[1])


def unpack_sum(returned, dest, gates):
    width = returned.shape[2]
    picked = returned.reshape(-1, width)[dest].reshape(gates.shape[0], gates.shape[1], width)
    return jnp.sum(gates[:, :, None] * picked.astype(jnp.float32), axis=1)


def body(
    fwd_prev,
    bwd_prev,
    stored_in,
    fwd_routes,
    fwd_gates,
    bwd_routes,
    bwd_gates,
    norm_gain,
    w_up,
    w_down,
):
    arriving = passed_along(fwd_prev, "segment", 1)[0]
    cotangent = passed_along(bwd_prev, "segment", -1)[0]
    gain = norm_gain[0]
    up_weight = w_up[0, 0]
    down_weight = w_down[0, 0]
    experts = lax.axis_size("expert")
    f_values, f_scale, f_normed = normalize(arriving, gain)
    b_values, b_scale, b_normed = normalize(stored_in[0], gain)
    f_dest = slot_index(fwd_routes[0], experts)
    b_dest = slot_index(bwd_routes[0], experts)
    f_buf = pack_rows(f_normed, f_dest, experts)
    b_buf = pack_rows(b_normed, b_dest, experts)
    c_buf = pack_rows(cotangent, b_dest, experts)
    rows_f = lax.all_to_all(f_buf, "expert", split_axis=0, concat_axis=0, tiled=True)
    rows_b = lax.all_to_all(b_buf, "expert", split_axis=0, concat_axis=0, tiled=True)
    rows_c = lax.all_to_all(c_buf, "expert", split_axis=0, concat_axis=0, tiled=True)
    shape = rows_f.shape
    out_f = expert_forward(rows_f.reshape(-1, shape[2]), up_weight, down_weight).reshape(shape)
    out_b = expert_backward(
        rows_b.reshape(-1, shape[2]), rows_c.reshape(-1, shape[2]), up_weight, down_weight
    ).reshape(shape)
    f_back = lax.all_to_all(out_f, "expert", split_axis=0, concat_axis=0, tiled=True)
    b_back = lax.all_to_all(out_b, "expert", split_axis=0, concat_axis=0, tiled=True)
    fwd_out = (f_values + unpack_sum(f_back, f_dest, fwd_gates[0])).astype(jnp.bfloat16)
    weighted = gain * unpack_sum(b_back, b_dest, bwd_gates[0])
    correction = b_values * b_scale**3 * jnp.mean(b_values * weighted, axis=-1, keepdims=True)
    bwd_out = (cotangent.astype(jnp.float32) + b_scale * weighted - correction).astype(jnp.bfloat16)
    return (fwd_out[None], bwd_out[None])


def solution(mesh):
    return jax.shard_map(
        body,
        mesh=mesh,
        in_specs=(
            P("segment", "expert", None),
            P("segment", "expert", None),
            P("segment", "expert", None),
            P("segment", "expert", None),
            P("segment", "expert", None),
            P("segment", "expert", None),
            P("segment", "expert", None),
            P("segment", None),
            P("segment", "expert", None, None),
            P("segment", "expert", None, None),
        ),
        out_specs=(P("segment", "expert", None), P("segment", "expert", None)),
        check_vma=False,
    )
```

profile of v0, /device:TPU:1, one launch (start us, length us, event | category | flops | bytes accessed | tf_op | source)
XLA Modules:
  0.0 288.6 jit_solution(10094154973611418066)
XLA Ops:
  0.6 0.8 copy.21
  1.6 0.7 broadcast_multiply_fusion
  2.3 0.6 reduce-window.16
  3.3 1.1 fusion.41
  4.4 0.7 reduce.1
  5.2 1.0 fusion.43
  6.7 3.2 %scatter_custom_fusion.2 = bf16[512,1536]{1,0:T(8,128)(2,1)} fusion(s32[256]{0:T(256)S(1)} %bitcast.128, bf16[256,1536]{1,0:T(8,128)(2,1)S(1)} %reshape.294, bf16[]{:T(256)} %constant.9.clone.1), kind=kCustom, calls=%fused_computation.22 | custom fusion | bytes 1572866 | tf_op jit(solution)/shard_map/scatter | solution.py:53
  9.9 12.9 %all-to-all-start.3 = ((bf16[32,16,1536]{2,1,0:T(8,128)(2,1)}), bf16[32,16,1536]{2,1,0:T(8,128)(2,1)S(1)}, u32[]{:S(2)}, u32[]{:S(2)}) async-start(bf16[32,16,1536]{2,1,0:T(8,128)(2,1)} %bitcast.20), calls=%async_computation.3 | async-start | bytes 3145728 | tf_op jit(solution)/shard_map/all_to_all | solution.py:89
  22.8 3.0 %collective-permute-start.1 = (bf16[1,64,1536]{2,1,0:T(8,128)(2,1)S(1)}, bf16[1,64,1536]{2,1,0:T(8,128)(2,1)S(1)}, u32[]{:S(2)}, u32[]{:S(2)}) collective-permute-start(bf16[1,64,1536]{2,1,0:T(8,128)(2,1)S(1)} %copy-done.4), channel_id=1, source_target_pairs={{0,224},{32,0},{64,32},{96,64},{128,96},{160,128},{192,160},{224,1... | collective-permute-start | bytes 589832 | tf_op jit(solution)/shard_map/ppermute | solution.py:16
  25.8 36.7 %collective-permute-done.1 = bf16[1,64,1536]{2,1,0:T(8,128)(2,1)S(1)} collective-permute-done((bf16[1,64,1536]{2,1,0:T(8,128)(2,1)S(1)}, bf16[1,64,1536]{2,1,0:T(8,128)(2,1)S(1)}, u32[]{:S(2)}, u32[]{:S(2)}) %collective-permute-start.1) | collective-permute-done | bytes 196640 | tf_op jit(solution)/shard_map/ppermute | solution.py:16
  62.9 3.1 %scatter_custom_fusion.1 = bf16[512,1536]{1,0:T(8,128)(2,1)} fusion(s32[256]{0:T(256)S(1)} %bitcast.129, bf16[256,1536]{1,0:T(8,128)(2,1)S(1)} %reshape.286, bf16[]{:T(256)} %constant.9.clone.1), kind=kCustom, calls=%fused_computation.24 | custom fusion | bytes 1572866 | tf_op jit(solution)/shard_map/scatter | solution.py:53
  66.0 9.7 %all-to-all-start.2 = ((bf16[32,16,1536]{2,1,0:T(8,128)(2,1)}), bf16[32,16,1536]{2,1,0:T(8,128)(2,1)}, u32[]{:S(2)}, u32[]{:S(2)}) async-start(bf16[32,16,1536]{2,1,0:T(8,128)(2,1)} %bitcast.18), calls=%async_computation.2 | async-start | bytes 3145728 | tf_op jit(solution)/shard_map/all_to_all | solution.py:90
  75.7 6.7 %fusion.6 = f32[512,1536]{1,0:T(8,128)} fusion(bf16[512,1536]{1,0:T(8,128)(2,1)S(1)} %bitcast.124, bf16[1,1,1536,1536]{3,2,1,0:T(8,128)(2,1)} %param.18), kind=kOutput, calls=%fused_computation.11 | convolution fusion | flops 2415919104 | bytes 9437184 | tf_op jit(solution)/shard_map/dot_general | solution.py:32
  82.4 25.1 %all-to-all-done.2 = bf16[32,16,1536]{2,1,0:T(8,128)(2,1)} async-done(((bf16[32,16,1536]{2,1,0:T(8,128)(2,1)}), bf16[32,16,1536]{2,1,0:T(8,128)(2,1)}, u32[]{:S(2)}, u32[]{:S(2)}) %all-to-all-start.2) | async-done | bytes 1572896 | tf_op jit(solution)/shard_map/all_to_all | solution.py:90
  107.5 7.0 %fusion.19 = bf16[512,1536]{1,0:T(8,128)(2,1)S(1)} fusion(f32[512,1536]{1,0:T(8,128)} %fusion.6, bf16[512,1536]{1,0:T(8,128)(2,1)} %bitcast.19, bf16[1,1,1536,1536]{3,2,1,0:T(8,128)(2,1)} %param.19), kind=kOutput, calls=%fused_computation.19 | convolution fusion | flops 2422996992 | bytes 11010048 | tf_op jit(solution)/shard_map/dot_general | solution.py:35
  114.5 3.8 %fusion.13 = bf16[512,1536]{1,0:T(8,128)(2,1)} fusion(bf16[512,1536]{1,0:T(8,128)(2,1)S(1)} %fusion.19, bf16[1,1,1536,1536]{3,2,1,0:T(8,128)(2,1)S(1)} %bitcast.138), kind=kOutput, calls=%fused_computation.17 | convolution fusion | flops 2416705536 | bytes 7864320 | tf_op jit(solution)/shard_map/dot_general | solution.py:39
  118.3 13.0 %all-to-all-start.4 = ((bf16[32,16,1536]{2,1,0:T(8,128)(2,1)}), bf16[32,16,1536]{2,1,0:T(8,128)(2,1)S(1)}, u32[]{:S(2)}, u32[]{:S(2)}) async-start(bf16[32,16,1536]{2,1,0:T(8,128)(2,1)} %bitcast.22), calls=%async_computation.4 | async-start | bytes 3145728 | tf_op jit(solution)/shard_map/all_to_all | solution.py:97
  131.3 2.2 collective-permute-start
  134.0 0.6 reduce-window.14
  135.1 38.4 %collective-permute-done = bf16[1,64,1536]{2,1,0:T(8,128)(2,1)S(1)} collective-permute-done((bf16[1,64,1536]{2,1,0:T(8,128)(2,1)S(1)}, bf16[1,64,1536]{2,1,0:T(8,128)(2,1)S(1)}, u32[]{:S(2)}, u32[]{:S(2)}) %collective-permute-start) | collective-permute-done | bytes 196640 | tf_op jit(solution)/shard_map/ppermute | solution.py:16
  173.7 1.3 gather_fusion.1
  174.9 0.5 reshape.257
  175.4 1.1 multiply_reduce_fusion
  177.1 2.3 scatter_custom_fusion
  179.4 49.3 %all_to_all.25 = bf16[32,16,1536]{2,1,0:T(8,128)(2,1)} all-to-all(bf16[32,16,1536]{2,1,0:T(8,128)(2,1)S(1)} %bitcast.123), channel_id=1, replica_groups=mesh['segment'=8,'expert'=32] {'expert'}, dimensions={0} | all-to-all | bytes 3145728 | tf_op jit(solution)/shard_map/all_to_all | solution.py:88
  228.8 10.7 %fusion.16 = bf16[512,1536]{1,0:T(8,128)(2,1)} fusion(bf16[1,1,1536,1536]{3,2,1,0:T(8,128)(2,1)} %param.19, bf16[512,1536]{1,0:T(8,128)(2,1)} %bitcast.126, bf16[1,1,1536,1536]{3,2,1,0:T(8,128)(2,1)} %param.18), kind=kOutput, calls=%fused_computation.18 | convolution fusion | flops 4836556800 | bytes 12582912 | tf_op jit(solution)/shard_map/dot_general | solution.py:28
  239.4 5.2 %all-to-all-start.1 = ((bf16[32,16,1536]{2,1,0:T(8,128)(2,1)}), bf16[32,16,1536]{2,1,0:T(8,128)(2,1)S(1)}, u32[]{:S(2)}, u32[]{:S(2)}) async-start(bf16[32,16,1536]{2,1,0:T(8,128)(2,1)} %bitcast.125), calls=%async_computation.1 | async-start | bytes 3145728 | tf_op jit(solution)/shard_map/all_to_all | solution.py:96
  244.8 40.0 %all-to-all-done.1 = bf16[32,16,1536]{2,1,0:T(8,128)(2,1)S(1)} async-done(((bf16[32,16,1536]{2,1,0:T(8,128)(2,1)}), bf16[32,16,1536]{2,1,0:T(8,128)(2,1)S(1)}, u32[]{:S(2)}, u32[]{:S(2)}) %all-to-all-start.1) | async-done | bytes 1572896 | tf_op jit(solution)/shard_map/all_to_all | solution.py:96
  284.8 1.3 gather_fusion
  286.1 0.5 reshape.255
  286.6 1.1 multiply_reduce_fusion.1
  287.7 1.0 fusion.40
  (56 shorter events, 3.3 us)
Async XLA Ops:
  9.9 12.9 %copy-start.4 = (bf16[1,64,1536]{2,1,0:T(8,128)(2,1)S(1)}, bf16[1,64,1536]{2,1,0:T(8,128)(2,1)}, u32[]{:S(2)}) copy-start(bf16[1,64,1536]{2,1,0:T(8,128)(2,1)} %param.11) | copy-start | bytes 589828
  9.9 56.2 %all-to-all-start.3 = ((bf16[32,16,1536]{2,1,0:T(8,128)(2,1)}), bf16[32,16,1536]{2,1,0:T(8,128)(2,1)S(1)}, u32[]{:S(2)}, u32[]{:S(2)}) async-start(bf16[32,16,1536]{2,1,0:T(8,128)(2,1)} %bitcast.20), calls=%async_computation.3 | async-start | bytes 3145728 | tf_op jit(solution)/shard_map/all_to_all | solution.py:89
  22.8 39.7 %collective-permute-start.1 = (bf16[1,64,1536]{2,1,0:T(8,128)(2,1)S(1)}, bf16[1,64,1536]{2,1,0:T(8,128)(2,1)S(1)}, u32[]{:S(2)}, u32[]{:S(2)}) collective-permute-start(bf16[1,64,1536]{2,1,0:T(8,128)(2,1)S(1)} %copy-done.4), channel_id=1, source_target_pairs={{0,224},{32,0},{64,32},{96,64},{128,96},{160,128},{192,160},{224,1... | collective-permute-start | bytes 589832 | tf_op jit(solution)/shard_map/ppermute | solution.py:16
  66.0 41.4 %all-to-all-start.2 = ((bf16[32,16,1536]{2,1,0:T(8,128)(2,1)}), bf16[32,16,1536]{2,1,0:T(8,128)(2,1)}, u32[]{:S(2)}, u32[]{:S(2)}) async-start(bf16[32,16,1536]{2,1,0:T(8,128)(2,1)} %bitcast.18), calls=%async_computation.2 | async-start | bytes 3145728 | tf_op jit(solution)/shard_map/all_to_all | solution.py:90
  75.7 38.7 %slice-start = ((s8[4718592]{0:T(1024)(128)(4,1)}), s8[524288]{0:T(1024)(128)(4,1)S(1)}, s32[]{:S(2)}) async-start(s8[4718592]{0:T(1024)(128)(4,1)} %bitcast.137), calls=%async_computation.5 | async-start | bytes 1048576
  107.5 7.0 %slice-start.1 = ((s8[4718592]{0:T(1024)(128)(4,1)}), s8[4194304]{0:T(1024)(128)(4,1)S(1)}, s32[]{:S(2)}) async-start(s8[4718592]{0:T(1024)(128)(4,1)} %bitcast.137), calls=%async_computation.6 | async-start | bytes 8388608
  118.3 13.0 %copy-start.5 = (bf16[1,64,1536]{2,1,0:T(8,128)(2,1)S(1)}, bf16[1,64,1536]{2,1,0:T(8,128)(2,1)}, u32[]{:S(2)}) copy-start(bf16[1,64,1536]{2,1,0:T(8,128)(2,1)} %param.10) | copy-start | bytes 589828
  118.3 15.3 %copy-start.1 = (s32[1,64,4]{1,2,0:T(4,128)S(1)}, s32[1,64,4]{1,2,0:T(4,128)}, u32[]{:S(2)}) copy-start(s32[1,64,4]{1,2,0:T(4,128)} %param.13) | copy-start | bytes 3076
  118.3 15.6 %copy-start.2 = (f32[1,64,4]{1,2,0:T(4,128)S(1)}, f32[1,64,4]{1,2,0:T(4,128)}, u32[]{:S(2)}) copy-start(f32[1,64,4]{1,2,0:T(4,128)} %param.16) | copy-start | bytes 3076
  118.3 55.4 %all-to-all-start.4 = ((bf16[32,16,1536]{2,1,0:T(8,128)(2,1)}), bf16[32,16,1536]{2,1,0:T(8,128)(2,1)S(1)}, u32[]{:S(2)}, u32[]{:S(2)}) async-start(bf16[32,16,1536]{2,1,0:T(8,128)(2,1)} %bitcast.22), calls=%async_computation.4 | async-start | bytes 3145728 | tf_op jit(solution)/shard_map/all_to_all | solution.py:97
  131.3 42.2 %collective-permute-start = (bf16[1,64,1536]{2,1,0:T(8,128)(2,1)S(1)}, bf16[1,64,1536]{2,1,0:T(8,128)(2,1)S(1)}, u32[]{:S(2)}, u32[]{:S(2)}) collective-permute-start(bf16[1,64,1536]{2,1,0:T(8,128)(2,1)S(1)} %copy-done.5), channel_id=1, source_target_pairs={{0,32},{32,64},{64,96},{96,128},{128,160},{160,192},{192,224},{224... | collective-permute-start | bytes 589832 | tf_op jit(solution)/shard_map/ppermute | solution.py:16
  175.4 1.1 copy-start
  239.4 5.2 %copy-start.3 = (f32[1,64,4]{1,2,0:T(4,128)S(1)}, f32[1,64,4]{1,2,0:T(4,128)}, u32[]{:S(2)}) copy-start(f32[1,64,4]{1,2,0:T(4,128)} %param.14) | copy-start | bytes 3076
  239.4 45.4 %all-to-all-start.1 = ((bf16[32,16,1536]{2,1,0:T(8,128)(2,1)}), bf16[32,16,1536]{2,1,0:T(8,128)(2,1)S(1)}, u32[]{:S(2)}, u32[]{:S(2)}) async-start(bf16[32,16,1536]{2,1,0:T(8,128)(2,1)} %bitcast.125), calls=%async_computation.1 | async-start | bytes 3145728 | tf_op jit(solution)/shard_map/all_to_all | solution.py:96
where the time goes:
time: 289 us
  waiting for transfers between devices  140 us (48%)
  blocking collectives  49.3 us (17%)
  starting transfers between devices  46 us (16%)
  matrix products  28.1 us (10%)
  local copies, waits for them, and re-layouts  15.6 us (5%)
  other arithmetic  8.47 us (3%)
    ppermute x2, waiting for transfers between devices, passed_along(): return lax.ppermute(value, axis, pairs)  75.1 us
    all_to_all x1, blocking collectives, body(): lax.all_to_all(f_buf, 'expert', split_axis=0, concat_axis=0, tiled=True)  49.3 us
    all_to_all x1, waiting for transfers between devices, body(): lax.all_to_all(out_f, 'expert', split_axis=0, concat_axis=0, tiled=True)  40 us
    all_to_all x1, waiting for transfers between devices, body(): lax.all_to_all(c_buf, 'expert', split_axis=0, concat_axis=0, tiled=True)  25.1 us
    all_to_all x1, starting transfers between devices, body(): lax.all_to_all(out_b, 'expert', split_axis=0, concat_axis=0, tiled=True)  13 us
    all_to_all x1, starting transfers between devices, body(): lax.all_to_all(b_buf, 'expert', split_axis=0, concat_axis=0, tiled=True)  12.9 us
    dot_general x1, matrix products, expert_forward(): jnp.dot(act, down_weight, preferred_element_type=jnp.float32)  10.7 us
    all_to_all x1, starting transfers between devices, body(): lax.all_to_all(c_buf, 'expert', split_axis=0, concat_axis=0, tiled=True)  9.67 us
  transfers between devices with their start and end apart: 6, of which 4 were waited for; matrix products, arithmetic and copies ran while one was open for 4% of the time, Pallas kernels for 0%

commit v1 on v0

v1 whole, which is shorter than its diff:
```python
import functools

import jax
import jax.numpy as jnp
from jax import lax
from jax.experimental import pallas as pl
from jax.experimental.pallas import tpu as pltpu
from jax.sharding import PartitionSpec as P

MESH = pl.DeviceIdType.MESH
TOK = 64
D = 1536
MOST = 16
SLOTS = 128
ROWS = 512
HALF = D // 2
TILE = 256
EPS = 1e-05

B, C, F = 0, 1, 2
OB_, OF_ = 0, 1
H0, H1 = (0, HALF), (HALF, HALF)
FULL = (0, D)


def kernel(
    fwd_ref,
    bwd_ref,
    stored_ref,
    meta_ref,
    gain_ref,
    up_hbm,
    down_hbm,
    fout_ref,
    bout_ref,
    up,
    down,
    meta,
    ag,
    fraw,
    sb,
    rx,
    mid,
    ob,
    rt,
    ps,
    fr,
    hs,
    acc,
    pt,
    ghi,
    glo,
    wsem,
    meta_s,
    meta_r,
    seg_s,
    ag_s,
    ag_r,
    y_s,
    rx_r,
    ret_s,
    rt_r,
    fr_s,
    fr_r,
    hs_s,
    hs_r,
):
    s = lax.axis_index("segment")
    e = lax.axis_index("expert")
    y, z, c = e // 8, (e // 2) % 4, e % 2
    g = 2 * (s % 2) - 1

    def at(dy, role, core, ds=0):
        return (
            (s + ds + 8) % 8,
            ((y + dy) % 4) * 8 + ((z + role * g + 4) % 4) * 2 + core,
        )

    def remote(src, dst, ssem, rsem, device):
        copy = pltpu.make_async_remote_copy(
            src_ref=src, dst_ref=dst, send_sem=ssem, recv_sem=rsem, device_id=device, device_id_type=MESH
        )
        copy.start()

    def wait(ref, sem):
        pltpu.make_async_copy(ref, ref, sem).wait()

    up_copy = pltpu.make_async_copy(up_hbm, up, wsem.at[0])
    down_copy = pltpu.make_async_copy(down_hbm, down, wsem.at[1])
    up_copy.start()
    down_copy.start()

    partners = [at(dy, 0, core) for dy in (1, 2, 3) for core in (0, 1)]
    partners += [at(0, 0, 1 - c), at(0, 1, c), at(0, -1, c), at(0, 2, c)]
    partners += [at(0, 0, c, 1), at(0, 1, c, 1), at(0, 0, c, -1), at(0, 1, c, -1)]
    barrier = pltpu.get_barrier_semaphore()
    for device in partners:
        pl.semaphore_signal(barrier, inc=1, device_id=device, device_id_type=MESH)

    gain = gain_ref[...]

    def scale_of(values):
        return lax.rsqrt(jnp.mean(values * values, axis=-1, keepdims=True) + EPS)

    def normalized(rows):
        values = rows.astype(jnp.float32)
        return (values * scale_of(values) * gain).astype(jnp.bfloat16)

    slot = lax.broadcasted_iota(jnp.int32, (SLOTS, SLOTS), 0)
    group = slot // MOST
    expert_of = (((y + group // 2) % 4) * 8 + z * 2 + group % 2).astype(jnp.float32)
    rank_of = (slot % MOST).astype(jnp.float32)
    before = (slot < lax.broadcasted_iota(jnp.int32, (SLOTS, SLOTS), 1)).astype(jnp.bfloat16)

    def places(which, role, gates):
        base = 8 * which
        chosen = jnp.zeros((SLOTS, SLOTS), jnp.float32)
        weight = jnp.zeros((SLOTS, SLOTS), jnp.float32)
        for k in range(4):
            same = (meta[role, base + k : base + k + 1, :] == expert_of).astype(jnp.float32)
            chosen += same
            if gates:
                weight += same * meta[role, base + 4 + k : base + 5 + k, :]
        rank = jnp.dot(chosen.astype(jnp.bfloat16), before, preferred_element_type=jnp.float32)
        placed = chosen * (rank == rank_of).astype(jnp.float32)
        return placed, weight

    def make_pack(which, role):
        placed, _ = places(which, role, False)
        pt[which, role] = placed.astype(jnp.bfloat16)

    def make_gates(which, role):
        placed, weight = places(which, role, True)
        gates = jnp.transpose(placed * weight)[:TOK]
        high = gates.astype(jnp.bfloat16)
        ghi[which, role] = high
        glo[which, role] = (gates - high.astype(jnp.float32)).astype(jnp.bfloat16)

    def pack(a, role, cols):
        which = 0 if a < F else 1
        sb[a, role * SLOTS : (role + 1) * SLOTS, pl.ds(*cols)] = jnp.dot(
            pt[which, role][:, :TOK], ag[a, role, :, pl.ds(*cols)], preferred_element_type=jnp.float32
        ).astype(jnp.bfloat16)

    def spread(src, dst, role, cols, ssem, rsem):
        def rows(k):
            return pl.ds(pl.multiple_of((role * 8 + k) * MOST, MOST), MOST)

        for dy in (2, 1, 3):
            for core in (0, 1):
                remote(
                    src.at[rows(dy * 2 + core), pl.ds(*cols)],
                    dst.at[rows((4 - dy) * 2 + c), pl.ds(*cols)],
                    ssem,
                    rsem,
                    at(dy, 0, core),
                )
        remote(src.at[rows(1 - c), pl.ds(*cols)], dst.at[rows(c), pl.ds(*cols)], ssem, rsem, at(0, 0, 1 - c))
        pltpu.make_async_copy(src.at[rows(c), pl.ds(*cols)], dst.at[rows(c), pl.ds(*cols)], rsem).start()

    def dispatch(a, role, cols):
        spread(sb.at[a], rx.at[a], role, cols, y_s.at[a], rx_r.at[a])

    def give_back(o, role, cols, part):
        spread(ob.at[o], rt.at[o], role, cols, ret_s.at[o], rt_r.at[o, role, part])

    meta[0] = meta_ref[...]
    ag[B, 0] = normalized(stored_ref[...])
    make_pack(0, 0)
    pack(B, 0, FULL)

    pl.semaphore_wait(barrier, len(partners))

    for i, role in enumerate((1, 3, 2)):
        remote(meta.at[0], meta.at[4 - role], meta_s.at[i], meta_r.at[4 - role], at(0, role, c))
    near, other = at(0, 1, c), at(0, -1, c)

    def half(ref, h):
        return ref.at[:, pl.ds(h * HALF, HALF)]

    for i, (role, h) in enumerate(((1, 0), (3, 1), (1, 1), (3, 0))):
        dest = near if role == 1 else other
        remote(half(ag.at[B, 0], h), half(ag.at[B, 4 - role], h), ag_s.at[B, i], ag_r.at[B, 4 - role, h], dest)
    dispatch(B, 0, FULL)

    for role in (3, 1, 2):
        wait(meta.at[role], meta_r.at[role])
        make_pack(0, role)

    def hop_b(role, h):
        wait(half(ag.at[B, role], h), ag_r.at[B, role, h])
        if (role, h) == (3, 0):
            remote(half(ag.at[B, 3], 0), half(ag.at[B, 2], 0), ag_s.at[B, 4], ag_r.at[B, 2, 0], near)
        if (role, h) == (1, 1):
            remote(half(ag.at[B, 1], 1), half(ag.at[B, 2], 1), ag_s.at[B, 5], ag_r.at[B, 2, 1], other)
        pack(B, role, (h * HALF, HALF))
        dispatch(B, role, (h * HALF, HALF))

    hop_b(3, 0)
    hop_b(1, 1)
    remote(bwd_ref, ag.at[C, 0], seg_s.at[0], ag_r.at[C, 0, 0], at(0, 0, c, -1))
    remote(bwd_ref, ag.at[C, 1], seg_s.at[1], ag_r.at[C, 1, 0], at(0, 1, c, -1))
    hop_b(3, 1)
    hop_b(1, 0)

    def hop(a, role):
        blocks = ag.at[C] if a == C else fraw
        wait(blocks.at[role], ag_r.at[a, role, 0])
        if role == 0:
            remote(blocks.at[0], blocks.at[3], ag_s.at[a, 0], ag_r.at[a, 3, 0], near)
        if role == 1:
            remote(blocks.at[1], blocks.at[2], ag_s.at[a, 1], ag_r.at[a, 2, 0], other)
        if a == F:
            ag[F, role] = normalized(fraw[role])
        pack(a, role, FULL)
        dispatch(a, role, FULL)

    for role in range(4):
        make_pack(1, role)
    hop(C, 0)
    hop(C, 1)
    hop_b(2, 0)
    hop_b(2, 1)
    remote(fwd_ref, fraw.at[0], seg_s.at[2], ag_r.at[F, 0, 0], at(0, 0, c, 1))
    remote(fwd_ref, fraw.at[1], seg_s.at[3], ag_r.at[F, 1, 0], at(0, 1, c, 1))
    for role in range(4):
        make_gates(0, role)
        make_gates(1, role)
    hop(C, 3)
    hop(C, 2)
    hop(F, 0)
    hop(F, 1)

    up_copy.wait()
    down_copy.wait()
    wait(rx.at[B], rx_r.at[B])
    wait(rx.at[C], rx_r.at[C])

    def tile(n):
        return pl.ds(pl.multiple_of(n * TILE, TILE), TILE)

    nt = (((1,), (1,)), ((), ()))

    def back_in(n, carry):
        pre = jnp.dot(rx[B], up[:, tile(n)], preferred_element_type=jnp.float32)
        sigma = jax.nn.sigmoid(pre)
        deriv = sigma * (1.0 + pre * (1.0 - sigma))
        back = lax.dot_general(rx[C], down[tile(n), :], nt, preferred_element_type=jnp.float32)
        mid[:, tile(n)] = (back * deriv).astype(jnp.bfloat16)
        return carry

    def back_out(n, carry):
        ob[OB_, :, tile(n)] = lax.dot_general(
            mid[...], up[tile(n), :], nt, preferred_element_type=jnp.float32
        ).astype(jnp.bfloat16)
        return carry

    def front_in(n, carry):
        pre = jnp.dot(rx[F], up[:, tile(n)], preferred_element_type=jnp.float32)
        mid[:, tile(n)] = jax.nn.silu(pre).astype(jnp.bfloat16)
        return carry

    def front_out(n, carry):
        ob[OF_, :, tile(n)] = jnp.dot(mid[...], down[:, tile(n)], preferred_element_type=jnp.float32).astype(
            jnp.bfloat16
        )
        return carry

    lax.fori_loop(0, 3, back_in, 0)
    hop(F, 3)
    lax.fori_loop(3, 6, back_in, 0)
    hop(F, 2)
    lax.fori_loop(0, 6, back_out, 0)

    give_back(OB_, 2, H0, 0)
    give_back(OB_, 2, H1, 1)
    give_back(OB_, 1, H0, 0)
    give_back(OB_, 3, H0, 0)
    give_back(OB_, 1, H1, 1)
    give_back(OB_, 3, H1, 1)
    give_back(OB_, 0, H0, 0)
    give_back(OB_, 0, H1, 1)

    wait(rx.at[F], rx_r.at[F])
    lax.fori_loop(0, 6, front_in, 0)
    lax.fori_loop(0, 6, front_out, 0)

    def gather(o, role, h):
        lane = pl.ds(h * HALF, HALF)
        block = rt.at[o, pl.ds(role * SLOTS, SLOTS), lane]
        wait(block, rt_r.at[o, role, h])
        rows = block[...]
        total = jnp.dot(ghi[o, role], rows, preferred_element_type=jnp.float32) + jnp.dot(
            glo[o, role], rows, preferred_element_type=jnp.float32
        )
        if role == 0:
            acc[o, :, lane] = total
            return
        if (role, h) in ((1, 0), (3, 1)):
            wait(half(fr.at[o], h), fr_r.at[o, h])
            total += fr[o, :, lane].astype(jnp.float32)
        ps[o, role, :, lane] = total.astype(jnp.bfloat16)
        if role == 2:
            remote(half(ps.at[o, 2], h), half(fr.at[o], h), fr_s.at[o, h], fr_r.at[o, h], near if h == 0 else other)
        else:
            i = 0 if role == 1 else 1
            remote(
                half(ps.at[o, role], h),
                half(hs.at[o, i], h),
                hs_s.at[o, i, h],
                hs_r.at[o, i, h],
                near if role == 1 else other,
            )

    def summed(o, h):
        lane = pl.ds(h * HALF, HALF)
        for i in (0, 1):
            wait(half(hs.at[o, i], h), hs_r.at[o, i, h])
        return acc[o, :, lane] + hs[o, 0, :, lane].astype(jnp.float32) + hs[o, 1, :, lane].astype(jnp.float32)

    gather(OB_, 2, 0)
    gather(OB_, 2, 1)
    give_back(OF_, 2, H0, 0)
    give_back(OF_, 2, H1, 1)
    gather(OB_, 1, 0)
    gather(OB_, 3, 0)
    give_back(OF_, 1, H0, 0)
    give_back(OF_, 3, H0, 0)
    gather(OB_, 1, 1)
    gather(OB_, 3, 1)
    give_back(OF_, 1, H1, 1)
    give_back(OF_, 3, H1, 1)
    gather(OB_, 0, 0)
    gather(OB_, 0, 1)
    give_back(OF_, 0, H0, 0)
    give_back(OF_, 0, H1, 1)
    gather(OF_, 2, 0)
    gather(OF_, 2, 1)

    for h in (0, 1):
        acc[OB_, :, pl.ds(h * HALF, HALF)] = summed(OB_, h)
    weighted = gain * acc[OB_]
    values = stored_ref[...].astype(jnp.float32)
    scale = scale_of(values)
    correction = values * (scale * scale * scale) * jnp.mean(values * weighted, axis=-1, keepdims=True)
    bout_ref[...] = (ag[C, 0].astype(jnp.float32) + scale * weighted - correction).astype(jnp.bfloat16)

    gather(OF_, 1, 0)
    gather(OF_, 3, 0)
    gather(OF_, 1, 1)
    gather(OF_, 3, 1)
    gather(OF_, 0, 0)
    gather(OF_, 0, 1)
    for h in (0, 1):
        lane = pl.ds(h * HALF, HALF)
        fout_ref[:, lane] = (fraw[0, :, lane].astype(jnp.float32) + summed(OF_, h)).astype(jnp.bfloat16)

    for i in range(3):
        wait(meta.at[0], meta_s.at[i])
    for i in range(4):
        wait(fraw.at[0], seg_s.at[i])
    for i in range(6):
        wait(half(ag.at[B, 0], 0), ag_s.at[B, i])
    for a in (C, F):
        for i in range(2):
            wait(ag.at[a, 0], ag_s.at[a, i])
    sent = pl.ds(0, ROWS * 7 // 8)
    for a in (B, C, F):
        wait(sb.at[a, sent], y_s.at[a])
    for o in (OB_, OF_):
        wait(ob.at[o, sent], ret_s.at[o])
        for h in (0, 1):
            wait(half(fr.at[o], h), fr_s.at[o, h])
            for i in (0, 1):
                wait(half(hs.at[o, i], h), hs_s.at[o, i, h])


def section(fwd_prev, bwd_prev, stored_in, fwd_routes, fwd_gates, bwd_routes, bwd_gates, norm_gain, w_up, w_down):
    lines = jnp.concatenate(
        [bwd_routes[0].astype(jnp.float32), bwd_gates[0], fwd_routes[0].astype(jnp.float32), fwd_gates[0]], axis=1
    ).T
    lines = jnp.pad(lines, ((0, 0), (0, SLOTS - TOK)), constant_values=-1.0)
    vmem = pl.BlockSpec(memory_space=pltpu.VMEM)
    anywhere = pl.BlockSpec(memory_space=pl.ANY)
    bf16, f32 = jnp.bfloat16, jnp.float32
    dma = pltpu.SemaphoreType.DMA
    out = jax.ShapeDtypeStruct((TOK, D), bf16)
    fwd_out, bwd_out = pl.pallas_call(
        kernel,
        out_shape=(out, out),
        in_specs=[vmem] * 5 + [anywhere] * 2,
        out_specs=(vmem, vmem),
        scratch_shapes=[
            pltpu.VMEM((D, D), bf16),
            pltpu.VMEM((D, D), bf16),
            pltpu.VMEM((4, 16, SLOTS), f32),
            pltpu.VMEM((3, 4, TOK, D), bf16),
            pltpu.VMEM((4, TOK, D), bf16),
            pltpu.VMEM((3, ROWS, D), bf16),
            pltpu.VMEM((3, ROWS, D), bf16),
            pltpu.VMEM((ROWS, D), bf16),
            pltpu.VMEM((2, ROWS, D), bf16),
            pltpu.VMEM((2, ROWS, D), bf16),
            pltpu.VMEM((2, 4, TOK, D), bf16),
            pltpu.VMEM((2, TOK, D), bf16),
            pltpu.VMEM((2, 2, TOK, D), bf16),
            pltpu.VMEM((2, TOK, D), f32),
            pltpu.VMEM((2, 4, SLOTS, SLOTS), bf16),
            pltpu.VMEM((2, 4, TOK, SLOTS), bf16),
            pltpu.VMEM((2, 4, TOK, SLOTS), bf16),
            dma((2,)),
            dma((3,)),
            dma((4,)),
            dma((4,)),
            dma((3, 6)),
            dma((3, 4, 2)),
            dma((3,)),
            dma((3,)),
            dma((2,)),
            dma((2, 4, 2)),
            dma((2, 2)),
            dma((2, 2)),
            dma((2, 2, 2)),
            dma((2, 2, 2)),
        ],
        compiler_params=pltpu.CompilerParams(collective_id=0, has_side_effects=True, vmem_limit_bytes=56 * 2**20),
        cost_estimate=pl.CostEstimate(
            flops=5 * 2 * ROWS * D * D, bytes_accessed=2 * D * D * 2 + 5 * TOK * D * 2, transcendentals=2 * ROWS * D
        ),
        name="section",
    )(fwd_prev[0], bwd_prev[0], stored_in[0], lines, norm_gain, w_up[0, 0], w_down[0, 0])
    return fwd_out[None], bwd_out[None]


def solution(mesh):
    block = P("segment", "expert", None)
    weight = P("segment", "expert", None, None)
    return jax.shard_map(
        section,
        mesh=mesh,
        in_specs=(block,) * 7 + (P("segment", None), weight, weight),
        out_specs=(block, block),
        check_vma=False,
    )
```

time: 289 us -> 116 us (0.40)
  waiting for transfers between devices: 140 us -> 0 us
  Pallas kernels: 0 us -> 109 us
  blocking collectives: 49.3 us -> 0 us
  starting transfers between devices: 46 us -> 0 us
  matrix products: 28.1 us -> 0 us
  local copies, waits for them, and re-layouts: 15.6 us -> 3.84 us
  other arithmetic: 8.47 us -> 1.41 us
    pallas_call x0 -> x1, Pallas kernels: none -> 109 us  [section(): pl.pallas_call(kernel, out_shape=(out, out), in_specs=[vmem] * 5 + [anywh...]
    ppermute x2 -> x0, waiting for transfers between devices: 75.1 us -> none  [passed_along(): return lax.ppermute(value, axis, pairs)]
    all_to_all x4 -> x0, waiting for transfers between devices: 65.1 us -> none  [the longest x1 40 us: body(): lax.all_to_all(out_f, 'expert', split_axis=0, concat_axis=0, tiled=True)]
    all_to_all x1 -> x0, blocking collectives: 49.3 us -> none  [body(): lax.all_to_all(f_buf, 'expert', split_axis=0, concat_axis=0, tiled=True)]
    all_to_all x4 -> x0, starting transfers between devices: 40.7 us -> none  [the longest x1 13 us: body(): lax.all_to_all(out_b, 'expert', split_axis=0, concat_axis=0, tiled=True)]
    dot_general x4 -> x0, matrix products: 28.1 us -> none  [the longest x1 10.7 us: expert_forward(): jnp.dot(act, down_weight, preferred_element_type=jnp.float32)]
    scatter x3 -> x0, local copies, waits for them, and re-layouts: 8.61 us -> none  [pack_rows(): buffer = buffer.at[dest].set(jnp.repeat(rows, TOP, axis=0))]
    ppermute x2 -> x0, starting transfers between devices: 5.25 us -> none  [passed_along(): return lax.ppermute(value, axis, pairs)]
  transfers between devices with their start and end apart: 6 -> 0, of which waited for: 4 -> 0; matrix products, arithmetic and copies ran while one was open for 4% -> 0% of each run, Pallas kernels for 0% -> 0%
where the time goes in v1:
time: 116 us; the launch traced here: 115 us
  Pallas kernels  109 us (94%)
  local copies, waits for them, and re-layouts  3.84 us (3%)
  other arithmetic  1.41 us (1%)
    pallas_call x1, Pallas kernels, section(): pl.pallas_call(kernel, out_shape=(out, out), in_specs=[vmem] * 5 + [anywh...  109 us
    unnamed x2, local copies, waits for them, and re-layouts  3.23 us

profile of v1, /device:TPU:1, one launch (start us, length us, event | category | flops | bytes accessed | tf_op | source)
XLA Modules:
  0.0 114.9 jit_solution(9111246926104259425)
XLA Ops:
  0.6 0.7 convert_bitcast_fusion
  1.3 0.7 maximum_bitcast_fusion
  2.0 0.6 pad.4.meta_ref
  2.6 109.0 %section.1 = (bf16[64,1536]{1,0:T(8,128)(2,1)}, bf16[64,1536]{1,0:T(8,128)(2,1)}) custom-call(bf16[64,1536]{1,0:T(8,128)(2,1)} %bitcast.21, bf16[64,1536]{1,0:T(8,128)(2,1)} %bitcast.22, bf16[64,1536]{1,0:T(8,128)(2,1)} %bitcast.23, f32[16,128]{1,0:T(8,128)} %pad.4.meta_ref, f32[1,1536]{1,0:T(1,128)} %gain_ref.1, bf16[1536,1536]{1,0:T(8,128)(2,1)} %bitcast.19, ...), custom_call_target="tpu_custom_call" | custom-call | flops 12079595520 | bytes 10420224 | tf_op jit(solution)/shard_map/section/pallas_call | solution.py:388
  111.6 1.6 %copy.14 = bf16[1,64,1536]{2,1,0:T(8,128)(2,1)} copy(bf16[1,64,1536]{2,1,0:T(8,128)(2,1)} %bitcast.16) | data formatting | bytes 393216
  113.3 1.6 %copy.15 = bf16[1,64,1536]{2,1,0:T(8,128)(2,1)} copy(bf16[1,64,1536]{2,1,0:T(8,128)(2,1)} %bitcast.15) | data formatting | bytes 393216

commit v2 on v1

--- a/solution.py
+++ b/solution.py
@@ -26,15 +26,24 @@
 def kernel(
     fwd_ref,
     bwd_ref,
-    stored_ref,
-    meta_ref,
-    gain_ref,
+    stored_hbm,
+    b_routes_hbm,
+    b_gates_hbm,
+    f_routes_hbm,
+    f_gates_hbm,
+    gain_hbm,
     up_hbm,
     down_hbm,
     fout_ref,
     bout_ref,
     up,
     down,
+    stored_ref,
+    b_routes_ref,
+    b_gates_ref,
+    f_routes_ref,
+    f_gates_ref,
+    gain_ref,
     meta,
     ag,
     fraw,
@@ -50,6 +59,7 @@
     pt,
     ghi,
     glo,
+    load_sem,
     wsem,
     meta_s,
     meta_r,
@@ -85,11 +95,6 @@
     def wait(ref, sem):
         pltpu.make_async_copy(ref, ref, sem).wait()
 
-    up_copy = pltpu.make_async_copy(up_hbm, up, wsem.at[0])
-    down_copy = pltpu.make_async_copy(down_hbm, down, wsem.at[1])
-    up_copy.start()
-    down_copy.start()
-
     partners = [at(dy, 0, core) for dy in (1, 2, 3) for core in (0, 1)]
     partners += [at(0, 0, 1 - c), at(0, 1, c), at(0, -1, c), at(0, 2, c)]
     partners += [at(0, 0, c, 1), at(0, 1, c, 1), at(0, 0, c, -1), at(0, 1, c, -1)]
@@ -97,14 +102,32 @@
     for device in partners:
         pl.semaphore_signal(barrier, inc=1, device_id=device, device_id_type=MESH)
 
-    gain = gain_ref[...]
+    loads = [
+        pltpu.make_async_copy(src, dst, load_sem.at[i])
+        for i, (src, dst) in enumerate(
+            (
+                (stored_hbm, stored_ref),
+                (b_routes_hbm, b_routes_ref),
+                (b_gates_hbm, b_gates_ref),
+                (f_routes_hbm, f_routes_ref),
+                (f_gates_hbm, f_gates_ref),
+                (gain_hbm, gain_ref),
+            )
+        )
+    ]
+    for load in loads:
+        load.start()
+    up_copy = pltpu.make_async_copy(up_hbm, up, wsem.at[0])
+    down_copy = pltpu.make_async_copy(down_hbm, down, wsem.at[1])
+    up_copy.start()
+    down_copy.start()
 
     def scale_of(values):
         return lax.rsqrt(jnp.mean(values * values, axis=-1, keepdims=True) + EPS)
 
     def normalized(rows):
         values = rows.astype(jnp.float32)
-        return (values * scale_of(values) * gain).astype(jnp.bfloat16)
+        return (values * scale_of(values) * gain_ref[...]).astype(jnp.bfloat16)
 
     slot = lax.broadcasted_iota(jnp.int32, (SLOTS, SLOTS), 0)
     group = slot // MOST
@@ -164,28 +187,35 @@
     def give_back(o, role, cols, part):
         spread(ob.at[o], rt.at[o], role, cols, ret_s.at[o], rt_r.at[o, role, part])
 
-    meta[0] = meta_ref[...]
+    near, other = at(0, 1, c), at(0, -1, c)
+
+    def half(ref, h):
+        return ref.at[:, pl.ds(h * HALF, HALF)]
+
+    def send_c(h):
+        for role in (0, 1):
+            remote(
+                half(bwd_ref, h), half(ag.at[C, role], h), seg_s.at[2 * h + role], ag_r.at[C, role, h], at(0, role, c, -1)
+            )
+
+    pl.semaphore_wait(barrier, len(partners))
+    send_c(0)
+    for load in loads:
+        load.wait()
+    meta[0] = jnp.full((16, SLOTS), -1.0, jnp.float32)
+    for i, ref in enumerate((b_routes_ref, b_gates_ref, f_routes_ref, f_gates_ref)):
+        meta[0, 4 * i : 4 * i + 4, :TOK] = ref[...].astype(jnp.float32)
+    for i, role in enumerate((1, 3, 2)):
+        remote(meta.at[0], meta.at[4 - role], meta_s.at[i], meta_r.at[4 - role], at(0, role, c))
+    send_c(1)
     ag[B, 0] = normalized(stored_ref[...])
     make_pack(0, 0)
     pack(B, 0, FULL)
-
-    pl.semaphore_wait(barrier, len(partners))
-
-    for i, role in enumerate((1, 3, 2)):
-        remote(meta.at[0], meta.at[4 - role], meta_s.at[i], meta_r.at[4 - role], at(0, role, c))
-    near, other = at(0, 1, c), at(0, -1, c)
-
-    def half(ref, h):
-        return ref.at[:, pl.ds(h * HALF, HALF)]
-
+    dispatch(B, 0, FULL)
     for i, (role, h) in enumerate(((1, 0), (3, 1), (1, 1), (3, 0))):
         dest = near if role == 1 else other
         remote(half(ag.at[B, 0], h), half(ag.at[B, 4 - role], h), ag_s.at[B, i], ag_r.at[B, 4 - role, h], dest)
-    dispatch(B, 0, FULL)
-
-    for role in (3, 1, 2):
-        wait(meta.at[role], meta_r.at[role])
-        make_pack(0, role)
+
 
     def hop_b(role, h):
         wait(half(ag.at[B, role], h), ag_r.at[B, role, h])
@@ -196,40 +226,51 @@
         pack(B, role, (h * HALF, HALF))
         dispatch(B, role, (h * HALF, HALF))
 
+    def hop_c(role, h):
+        wait(half(ag.at[C, role], h), ag_r.at[C, role, h])
+        if role == 0:
+            remote(half(ag.at[C, 0], h), half(ag.at[C, 3], h), ag_s.at[C, h], ag_r.at[C, 3, h], near)
+        if role == 1:
+            remote(half(ag.at[C, 1], h), half(ag.at[C, 2], h), ag_s.at[C, 2 + h], ag_r.at[C, 2, h], other)
+        pack(C, role, (h * HALF, HALF))
+        dispatch(C, role, (h * HALF, HALF))
+
+    def hop_f(role):
+        wait(fraw.at[role], ag_r.at[F, role, 0])
+        if role == 0:
+            remote(fraw.at[0], fraw.at[3], ag_s.at[F, 0], ag_r.at[F, 3, 0], near)
+        if role == 1:
+            remote(fraw.at[1], fraw.at[2], ag_s.at[F, 1], ag_r.at[F, 2, 0], other)
+        ag[F, role] = normalized(fraw[role])
+        pack(F, role, FULL)
+        dispatch(F, role, FULL)
+
+    hop_c(0, 0)
+    for role in (1, 3, 2):
+        wait(meta.at[role], meta_r.at[role])
+        make_pack(0, role)
+    hop_c(1, 0)
+    hop_c(0, 1)
+    hop_c(1, 1)
     hop_b(3, 0)
     hop_b(1, 1)
-    remote(bwd_ref, ag.at[C, 0], seg_s.at[0], ag_r.at[C, 0, 0], at(0, 0, c, -1))
-    remote(bwd_ref, ag.at[C, 1], seg_s.at[1], ag_r.at[C, 1, 0], at(0, 1, c, -1))
+    for role in (0, 1):
+        remote(fwd_ref, fraw.at[role], seg_s.at[4 + role], ag_r.at[F, role, 0], at(0, role, c, 1))
     hop_b(3, 1)
     hop_b(1, 0)
-
-    def hop(a, role):
-        blocks = ag.at[C] if a == C else fraw
-        wait(blocks.at[role], ag_r.at[a, role, 0])
-        if role == 0:
-            remote(blocks.at[0], blocks.at[3], ag_s.at[a, 0], ag_r.at[a, 3, 0], near)
-        if role == 1:
-            remote(blocks.at[1], blocks.at[2], ag_s.at[a, 1], ag_r.at[a, 2, 0], other)
-        if a == F:
-            ag[F, role] = normalized(fraw[role])
-        pack(a, role, FULL)
-        dispatch(a, role, FULL)
-
     for role in range(4):
         make_pack(1, role)
-    hop(C, 0)
-    hop(C, 1)
+    hop_c(3, 0)
+    hop_c(2, 0)
+    hop_c(3, 1)
+    hop_c(2, 1)
     hop_b(2, 0)
     hop_b(2, 1)
-    remote(fwd_ref, fraw.at[0], seg_s.at[2], ag_r.at[F, 0, 0], at(0, 0, c, 1))
-    remote(fwd_ref, fraw.at[1], seg_s.at[3], ag_r.at[F, 1, 0], at(0, 1, c, 1))
     for role in range(4):
         make_gates(0, role)
         make_gates(1, role)
-    hop(C, 3)
-    hop(C, 2)
-    hop(F, 0)
-    hop(F, 1)
+    hop_f(0)
+    hop_f(1)
 
     up_copy.wait()
     down_copy.wait()
@@ -267,9 +308,9 @@
         return carry
 
     lax.fori_loop(0, 3, back_in, 0)
-    hop(F, 3)
+    hop_f(3)
+    hop_f(2)
     lax.fori_loop(3, 6, back_in, 0)
-    hop(F, 2)
     lax.fori_loop(0, 6, back_out, 0)
 
     give_back(OB_, 2, H0, 0)
@@ -278,8 +319,6 @@
     give_back(OB_, 3, H0, 0)
     give_back(OB_, 1, H1, 1)
     give_back(OB_, 3, H1, 1)
-    give_back(OB_, 0, H0, 0)
-    give_back(OB_, 0, H1, 1)
 
     wait(rx.at[F], rx_r.at[F])
     lax.fori_loop(0, 6, front_in, 0)
@@ -320,8 +359,8 @@
 
     gather(OB_, 2, 0)
     gather(OB_, 2, 1)
-    give_back(OF_, 2, H0, 0)
-    give_back(OF_, 2, H1, 1)
+    for part, cols in enumerate((H0, H1)):
+        give_back(OF_, 2, cols, part)
     gather(OB_, 1, 0)
     gather(OB_, 3, 0)
     give_back(OF_, 1, H0, 0)
@@ -330,40 +369,40 @@
     gather(OB_, 3, 1)
     give_back(OF_, 1, H1, 1)
     give_back(OF_, 3, H1, 1)
+    for o in (OB_, OF_):
+        for part, cols in enumerate((H0, H1)):
+            give_back(o, 0, cols, part)
+    gather(OF_, 2, 0)
+    gather(OF_, 2, 1)
+    gather(OF_, 1, 0)
+    gather(OF_, 3, 0)
+    gather(OF_, 1, 1)
+    gather(OF_, 3, 1)
     gather(OB_, 0, 0)
     gather(OB_, 0, 1)
-    give_back(OF_, 0, H0, 0)
-    give_back(OF_, 0, H1, 1)
-    gather(OF_, 2, 0)
-    gather(OF_, 2, 1)
-
     for h in (0, 1):
         acc[OB_, :, pl.ds(h * HALF, HALF)] = summed(OB_, h)
-    weighted = gain * acc[OB_]
+    weighted = gain_ref[...] * acc[OB_]
     values = stored_ref[...].astype(jnp.float32)
     scale = scale_of(values)
     correction = values * (scale * scale * scale) * jnp.mean(values * weighted, axis=-1, keepdims=True)
     bout_ref[...] = (ag[C, 0].astype(jnp.float32) + scale * weighted - correction).astype(jnp.bfloat16)
 
-    gather(OF_, 1, 0)
-    gather(OF_, 3, 0)
-    gather(OF_, 1, 1)
-    gather(OF_, 3, 1)
-    gather(OF_, 0, 0)
-    gather(OF_, 0, 1)
     for h in (0, 1):
+        gather(OF_, 0, h)
         lane = pl.ds(h * HALF, HALF)
         fout_ref[:, lane] = (fraw[0, :, lane].astype(jnp.float32) + summed(OF_, h)).astype(jnp.bfloat16)
 
     for i in range(3):
         wait(meta.at[0], meta_s.at[i])
     for i in range(4):
-        wait(fraw.at[0], seg_s.at[i])
+        wait(half(ag.at[C, 0], 0), seg_s.at[i])
+        wait(half(ag.at[C, 0], 0), ag_s.at[C, i])
     for i in range(6):
         wait(half(ag.at[B, 0], 0), ag_s.at[B, i])
-    for a in (C, F):
-        for i in range(2):
-            wait(ag.at[a, 0], ag_s.at[a, i])
+    for i in range(2):
+        wait(fraw.at[0], seg_s.at[4 + i])
+        wait(fraw.at[0], ag_s.at[F, i])
     sent = pl.ds(0, ROWS * 7 // 8)
     for a in (B, C, F):
         wait(sb.at[a, sent], y_s.at[a])
@@ -375,24 +414,36 @@
                 wait(half(hs.at[o, i], h), hs_s.at[o, i, h])
 
 
+def finish(fwd_ref, bwd_ref, fout_ref, bout_ref, sem):
+    first = pltpu.make_async_copy(fwd_ref, fout_ref, sem.at[0])
+    second = pltpu.make_async_copy(bwd_ref, bout_ref, sem.at[1])
+    first.start()
+    second.start()
+    first.wait()
+    second.wait()
+
+
 def section(fwd_prev, bwd_prev, stored_in, fwd_routes, fwd_gates, bwd_routes, bwd_gates, norm_gain, w_up, w_down):
-    lines = jnp.concatenate(
-        [bwd_routes[0].astype(jnp.float32), bwd_gates[0], fwd_routes[0].astype(jnp.float32), fwd_gates[0]], axis=1
-    ).T
-    lines = jnp.pad(lines, ((0, 0), (0, SLOTS - TOK)), constant_values=-1.0)
     vmem = pl.BlockSpec(memory_space=pltpu.VMEM)
     anywhere = pl.BlockSpec(memory_space=pl.ANY)
     bf16, f32 = jnp.bfloat16, jnp.float32
     dma = pltpu.SemaphoreType.DMA
     out = jax.ShapeDtypeStruct((TOK, D), bf16)
+    kept = pltpu.VMEM((TOK, D), bf16)
     fwd_out, bwd_out = pl.pallas_call(
         kernel,
-        out_shape=(out, out),
-        in_specs=[vmem] * 5 + [anywhere] * 2,
+        out_shape=(kept, kept),
+        in_specs=[anywhere] * 10,
         out_specs=(vmem, vmem),
         scratch_shapes=[
             pltpu.VMEM((D, D), bf16),
             pltpu.VMEM((D, D), bf16),
+            pltpu.VMEM((TOK, D), bf16),
+            pltpu.VMEM((4, TOK), jnp.int32),
+            pltpu.VMEM((4, TOK), f32),
+            pltpu.VMEM((4, TOK), jnp.int32),
+            pltpu.VMEM((4, TOK), f32),
+            pltpu.VMEM((1, D), f32),
             pltpu.VMEM((4, 16, SLOTS), f32),
             pltpu.VMEM((3, 4, TOK, D), bf16),
             pltpu.VMEM((4, TOK, D), bf16),
@@ -408,10 +459,11 @@
             pltpu.VMEM((2, 4, SLOTS, SLOTS), bf16),
             pltpu.VMEM((2, 4, TOK, SLOTS), bf16),
             pltpu.VMEM((2, 4, TOK, SLOTS), bf16),
+            dma((6,)),
             dma((2,)),
             dma((3,)),
             dma((4,)),
-            dma((4,)),
+            dma((6,)),
             dma((3, 6)),
             dma((3, 4, 2)),
             dma((3,)),
@@ -428,7 +480,26 @@
             flops=5 * 2 * ROWS * D * D, bytes_accessed=2 * D * D * 2 + 5 * TOK * D * 2, transcendentals=2 * ROWS * D
         ),
         name="section",
-    )(fwd_prev[0], bwd_prev[0], stored_in[0], lines, norm_gain, w_up[0, 0], w_down[0, 0])
+    )(
+        fwd_prev[0],
+        bwd_prev[0],
+        stored_in[0],
+        bwd_routes[0].T,
+        bwd_gates[0].T,
+        fwd_routes[0].T,
+        fwd_gates[0].T,
+        norm_gain,
+        w_up[0, 0],
+        w_down[0, 0],
+    )
+    fwd_out, bwd_out = pl.pallas_call(
+        finish,
+        out_shape=(out, out),
+        in_specs=[vmem] * 2,
+        out_specs=(anywhere, anywhere),
+        scratch_shapes=[dma((2,))],
+        name="finish",
+    )(*(pltpu.with_memory_space_constraint(v, pltpu.VMEM) for v in (fwd_out, bwd_out)))
     return fwd_out[None], bwd_out[None]
 
 

time: 116 us -> 111 us (0.957)
  the two profiles are of different devices: /device:TPU:1 before, /device:TPU:42 now
where the time goes in v2:
time: 111 us
  Pallas kernels  110 us (99%)
    pallas_call x1, Pallas kernels, section(): pl.pallas_call(kernel, out_shape=(kept, kept), in_specs=[anywhere] * 10,...  109 us

profile of v2, /device:TPU:42, one launch (start us, length us, event | category | flops | bytes accessed | tf_op | source)
XLA Modules:
  0.0 110.7 jit_solution(2562794338619783688)
XLA Ops:
  0.6 109.3 %section.1 = (bf16[64,1536]{1,0:T(8,128)(2,1)S(1)}, bf16[64,1536]{1,0:T(8,128)(2,1)S(1)}) custom-call(bf16[64,1536]{1,0:T(8,128)(2,1)} %bitcast.21, bf16[64,1536]{1,0:T(8,128)(2,1)} %bitcast.22, bf16[64,1536]{1,0:T(8,128)(2,1)} %bitcast.23, s32[4,64]{1,0:T(4,128)} %bitcast.26, f32[4,64]{1,0:T(4,128)} %bitcast.27, s32[4,64]{1,0:T(4,128)} %bitcast.28, ...), custom_call_target="tpu_custom_call" | custom-call | flops 12079595520 | bytes 10420224 | tf_op jit(solution)/shard_map/section/pallas_call | solution.py:433
  109.9 0.8 finish.1

commit v3 on v2

--- a/solution.py
+++ b/solution.py
@@ -208,6 +208,8 @@
     for i, role in enumerate((1, 3, 2)):
         remote(meta.at[0], meta.at[4 - role], meta_s.at[i], meta_r.at[4 - role], at(0, role, c))
     send_c(1)
+    for role in (0, 1):
+        remote(fwd_ref, fraw.at[role], seg_s.at[4 + role], ag_r.at[F, role, 0], at(0, role, c, 1))
     ag[B, 0] = normalized(stored_ref[...])
     make_pack(0, 0)
     pack(B, 0, FULL)
@@ -228,10 +230,6 @@
 
     def hop_c(role, h):
         wait(half(ag.at[C, role], h), ag_r.at[C, role, h])
-        if role == 0:
-            remote(half(ag.at[C, 0], h), half(ag.at[C, 3], h), ag_s.at[C, h], ag_r.at[C, 3, h], near)
-        if role == 1:
-            remote(half(ag.at[C, 1], h), half(ag.at[C, 2], h), ag_s.at[C, 2 + h], ag_r.at[C, 2, h], other)
         pack(C, role, (h * HALF, HALF))
         dispatch(C, role, (h * HALF, HALF))
 
@@ -252,30 +250,31 @@
     hop_c(1, 0)
     hop_c(0, 1)
     hop_c(1, 1)
+    make_pack(1, 0)
+    make_pack(1, 1)
+    hop_f(0)
+    hop_f(1)
+    for h in (0, 1):
+        remote(half(ag.at[C, 0], h), half(ag.at[C, 3], h), ag_s.at[C, h], ag_r.at[C, 3, h], near)
+        remote(half(ag.at[C, 1], h), half(ag.at[C, 2], h), ag_s.at[C, 2 + h], ag_r.at[C, 2, h], other)
     hop_b(3, 0)
     hop_b(1, 1)
-    for role in (0, 1):
-        remote(fwd_ref, fraw.at[role], seg_s.at[4 + role], ag_r.at[F, role, 0], at(0, role, c, 1))
     hop_b(3, 1)
     hop_b(1, 0)
+    make_pack(1, 3)
+    make_pack(1, 2)
     for role in range(4):
-        make_pack(1, role)
+        make_gates(1, role)
+        make_gates(0, role)
+    hop_f(3)
+    hop_f(2)
     hop_c(3, 0)
     hop_c(2, 0)
     hop_c(3, 1)
     hop_c(2, 1)
     hop_b(2, 0)
     hop_b(2, 1)
-    for role in range(4):
-        make_gates(0, role)
-        make_gates(1, role)
-    hop_f(0)
-    hop_f(1)
-
-    up_copy.wait()
-    down_copy.wait()
-    wait(rx.at[B], rx_r.at[B])
-    wait(rx.at[C], rx_r.at[C])
+
 
     def tile(n):
         return pl.ds(pl.multiple_of(n * TILE, TILE), TILE)
@@ -306,23 +305,6 @@
             jnp.bfloat16
         )
         return carry
-
-    lax.fori_loop(0, 3, back_in, 0)
-    hop_f(3)
-    hop_f(2)
-    lax.fori_loop(3, 6, back_in, 0)
-    lax.fori_loop(0, 6, back_out, 0)
-
-    give_back(OB_, 2, H0, 0)
-    give_back(OB_, 2, H1, 1)
-    give_back(OB_, 1, H0, 0)
-    give_back(OB_, 3, H0, 0)
-    give_back(OB_, 1, H1, 1)
-    give_back(OB_, 3, H1, 1)
-
-    wait(rx.at[F], rx_r.at[F])
-    lax.fori_loop(0, 6, front_in, 0)
-    lax.fori_loop(0, 6, front_out, 0)
 
     def gather(o, role, h):
         lane = pl.ds(h * HALF, HALF)
@@ -357,27 +339,44 @@
             wait(half(hs.at[o, i], h), hs_r.at[o, i, h])
         return acc[o, :, lane] + hs[o, 0, :, lane].astype(jnp.float32) + hs[o, 1, :, lane].astype(jnp.float32)
 
-    gather(OB_, 2, 0)
-    gather(OB_, 2, 1)
-    for part, cols in enumerate((H0, H1)):
-        give_back(OF_, 2, cols, part)
-    gather(OB_, 1, 0)
-    gather(OB_, 3, 0)
-    give_back(OF_, 1, H0, 0)
-    give_back(OF_, 3, H0, 0)
-    gather(OB_, 1, 1)
-    gather(OB_, 3, 1)
-    give_back(OF_, 1, H1, 1)
-    give_back(OF_, 3, H1, 1)
-    for o in (OB_, OF_):
+    def give_back_sides(o):
         for part, cols in enumerate((H0, H1)):
-            give_back(o, 0, cols, part)
+            give_back(o, 1, cols, part)
+            give_back(o, 3, cols, part)
+
+    up_copy.wait()
+    down_copy.wait()
+    wait(rx.at[F], rx_r.at[F])
+    lax.fori_loop(0, 6, front_in, 0)
+    lax.fori_loop(0, 6, front_out, 0)
+    give_back(OF_, 2, H0, 0)
+    give_back(OF_, 2, H1, 1)
+    give_back_sides(OF_)
+
+    wait(rx.at[B], rx_r.at[B])
+    wait(rx.at[C], rx_r.at[C])
+    lax.fori_loop(0, 3, back_in, 0)
     gather(OF_, 2, 0)
     gather(OF_, 2, 1)
+    lax.fori_loop(3, 6, back_in, 0)
+    lax.fori_loop(0, 3, back_out, 0)
+    give_back(OB_, 2, H0, 0)
+    lax.fori_loop(3, 6, back_out, 0)
+    give_back(OB_, 2, H1, 1)
     gather(OF_, 1, 0)
     gather(OF_, 3, 0)
     gather(OF_, 1, 1)
     gather(OF_, 3, 1)
+    give_back_sides(OB_)
+    gather(OB_, 2, 0)
+    gather(OB_, 2, 1)
+    for o in (OB_, OF_):
+        for part, cols in enumerate((H0, H1)):
+            give_back(o, 0, cols, part)
+    gather(OB_, 1, 0)
+    gather(OB_, 3, 0)
+    gather(OB_, 1, 1)
+    gather(OB_, 3, 1)
     gather(OB_, 0, 0)
     gather(OB_, 0, 1)
     for h in (0, 1):

time: 111 us -> 108 us (0.973)
  the two profiles are of different devices: /device:TPU:42 before, /device:TPU:10 now
where the time goes in v3:
time: 108 us
  Pallas kernels  107 us (99%)
    pallas_call x1, Pallas kernels, section(): pl.pallas_call(kernel, out_shape=(kept, kept), in_specs=[anywhere] * 10,...  106 us

profile of v3, /device:TPU:10, one launch (start us, length us, event | category | flops | bytes accessed | tf_op | source)
XLA Modules:
  0.0 107.6 jit_solution(8358248037167880549)
XLA Ops:
  0.6 106.2 %section.1 = (bf16[64,1536]{1,0:T(8,128)(2,1)S(1)}, bf16[64,1536]{1,0:T(8,128)(2,1)S(1)}) custom-call(bf16[64,1536]{1,0:T(8,128)(2,1)} %bitcast.21, bf16[64,1536]{1,0:T(8,128)(2,1)} %bitcast.22, bf16[64,1536]{1,0:T(8,128)(2,1)} %bitcast.23, s32[4,64]{1,0:T(4,128)} %bitcast.26, f32[4,64]{1,0:T(4,128)} %bitcast.27, s32[4,64]{1,0:T(4,128)} %bitcast.28, ...), custom_call_target="tpu_custom_call" | custom-call | flops 12079595520 | bytes 10420224 | tf_op jit(solution)/shard_map/section/pallas_call | solution.py:432
  106.8 0.8 finish.1

commit v4 on v3

--- a/solution.py
+++ b/solution.py
@@ -359,12 +359,12 @@
     gather(OF_, 2, 0)
     gather(OF_, 2, 1)
     lax.fori_loop(3, 6, back_in, 0)
+    gather(OF_, 1, 0)
+    gather(OF_, 3, 0)
     lax.fori_loop(0, 3, back_out, 0)
     give_back(OB_, 2, H0, 0)
     lax.fori_loop(3, 6, back_out, 0)
     give_back(OB_, 2, H1, 1)
-    gather(OF_, 1, 0)
-    gather(OF_, 3, 0)
     gather(OF_, 1, 1)
     gather(OF_, 3, 1)
     give_back_sides(OB_)

time: 108 us -> 106 us (0.981)
  the two profiles are of different devices: /device:TPU:10 before, /device:TPU:1 now
where the time goes in v4:
time: 106 us
  Pallas kernels  105 us (99%)
    pallas_call x1, Pallas kernels, section(): pl.pallas_call(kernel, out_shape=(kept, kept), in_specs=[anywhere] * 10,...  105 us

profile of v4, /device:TPU:1, one launch (start us, length us, event | category | flops | bytes accessed | tf_op | source)
XLA Modules:
  0.0 105.9 jit_solution(676996449373477425)
XLA Ops:
  0.6 104.5 %section.1 = (bf16[64,1536]{1,0:T(8,128)(2,1)S(1)}, bf16[64,1536]{1,0:T(8,128)(2,1)S(1)}) custom-call(bf16[64,1536]{1,0:T(8,128)(2,1)} %bitcast.21, bf16[64,1536]{1,0:T(8,128)(2,1)} %bitcast.22, bf16[64,1536]{1,0:T(8,128)(2,1)} %bitcast.23, s32[4,64]{1,0:T(4,128)} %bitcast.26, f32[4,64]{1,0:T(4,128)} %bitcast.27, s32[4,64]{1,0:T(4,128)} %bitcast.28, ...), custom_call_target="tpu_custom_call" | custom-call | flops 12079595520 | bytes 10420224 | tf_op jit(solution)/shard_map/section/pallas_call | solution.py:432
  105.2 0.8 finish.1

commit v5 on v4

--- a/solution.py
+++ b/solution.py
@@ -244,9 +244,8 @@
         dispatch(F, role, FULL)
 
     hop_c(0, 0)
-    for role in (1, 3, 2):
-        wait(meta.at[role], meta_r.at[role])
-        make_pack(0, role)
+    wait(meta.at[1], meta_r.at[1])
+    make_pack(0, 1)
     hop_c(1, 0)
     hop_c(0, 1)
     hop_c(1, 1)
@@ -257,10 +256,14 @@
     for h in (0, 1):
         remote(half(ag.at[C, 0], h), half(ag.at[C, 3], h), ag_s.at[C, h], ag_r.at[C, 3, h], near)
         remote(half(ag.at[C, 1], h), half(ag.at[C, 2], h), ag_s.at[C, 2 + h], ag_r.at[C, 2, h], other)
+    wait(meta.at[3], meta_r.at[3])
+    make_pack(0, 3)
     hop_b(3, 0)
     hop_b(1, 1)
     hop_b(3, 1)
     hop_b(1, 0)
+    wait(meta.at[2], meta_r.at[2])
+    make_pack(0, 2)
     make_pack(1, 3)
     make_pack(1, 2)
     for role in range(4):

time: 106 us -> 106 us (level)
  no operation moved by 1% of the time
where the time goes in v5:
time: 106 us
  Pallas kernels  105 us (99%)
    pallas_call x1, Pallas kernels, section(): pl.pallas_call(kernel, out_shape=(kept, kept), in_specs=[anywhere] * 10,...  105 us

profile of v5, /device:TPU:1, one launch (start us, length us, event | category | flops | bytes accessed | tf_op | source)
XLA Modules:
  0.0 105.9 jit_solution(2627605113985120927)
XLA Ops:
  0.6 104.5 %section.1 = (bf16[64,1536]{1,0:T(8,128)(2,1)S(1)}, bf16[64,1536]{1,0:T(8,128)(2,1)S(1)}) custom-call(bf16[64,1536]{1,0:T(8,128)(2,1)} %bitcast.21, bf16[64,1536]{1,0:T(8,128)(2,1)} %bitcast.22, bf16[64,1536]{1,0:T(8,128)(2,1)} %bitcast.23, s32[4,64]{1,0:T(4,128)} %bitcast.26, f32[4,64]{1,0:T(4,128)} %bitcast.27, s32[4,64]{1,0:T(4,128)} %bitcast.28, ...), custom_call_target="tpu_custom_call" | custom-call | flops 12079595520 | bytes 10420224 | tf_op jit(solution)/shard_map/section/pallas_call | solution.py:435
  105.2 0.8 finish.1
